TPU v7x, 256 devices: a whole 4x4x8 slice. The times are simulated.
256 devices in a mesh: rows: 32 (over z_hi, y, core), rep: 8 (over x, z_lo).
Axes of the slice: x: 4, y: 4, z: 8 (z_hi: 4, z_lo: 2; z = z_hi * 2 + z_lo), core: 2. Of those that a mesh axis runs over, the one named last changes fastest.
Arguments:
- features: bfloat16 [32768, 256], P('rows'), as said below
- weight: bfloat16 [256, 256], replicated, may hold values from -0.375 to 0.375
- cotangent: bfloat16 [32768, 256], P('rows'), may hold values from -6 to 6
- node_order: int32 [32, 1024], P('rows'), may hold values from 0 to 1023, each once within a row
- forward_tiles: bfloat16 [32, 8, 4, 32, 128, 128], P('rows', 'rep'), as said below
- forward_slots: int32 [32, 8, 4, 2, 32], P('rows', 'rep'), may hold values from 0 to 7, as said below
- forward_count: int32 [32, 8, 4], P('rows', 'rep'), may hold values from 1 to 32, as said below
- backward_tiles: bfloat16 [32, 8, 4, 32, 128, 128], P('rows', 'rep'), as said below
- backward_slots: int32 [32, 8, 4, 2, 32], P('rows', 'rep'), may hold values from 0 to 7, as said below
- backward_count: int32 [32, 8, 4], P('rows', 'rep'), may hold values from 1 to 32, as said below
Outputs:
- layer_output: bfloat16 [32768, 256], P('rows')
- grad_weight: float32 [256, 256], replicated
- grad_input: bfloat16 [32768, 256], P('rows')
Inputs may be any that keep to these rules, and one draw needn't show every extreme that they name: `node_order`: each row names every position of its row block once. forward_slots[i, r, t, 0, s] and forward_slots[i, r, t, 1, s] are the row tile and the column tile of slot s of the pair of row block i and column block t * 8 + r; the 32 slots of one pair name distinct tiles. `forward_count`: at most 32 live slots a pair, exactly 32 for some pair. `forward_tiles`: slots at or beyond a pair's count hold values that are not part of the operator. backward_tiles[j, r, t, s] is forward_tiles[i, j % 8, j // 8, s] transposed, with i = t * 8 + r. backward_slots[j, r, t, 0, s] = forward_slots[i, j % 8, j // 8, 1, s] and backward_slots[j, r, t, 1, s] = forward_slots[i, j % 8, j // 8, 0, s], with i = t * 8 + r. backward_count[j, r, t] = forward_count[i, j % 8, j // 8], with i = t * 8 + r. `features`: nonnegative.
All inputs are finite; a program needn't handle non-finite values.
Results may differ from a plain program's by a relative error of at most 0.0051.
Values may be sent and summed in bfloat16 or wider, within the bound.
A program may use at most 128 MiB of HBM per device.

v0:
```python
import math

import jax
import jax.numpy as jnp
from jax import lax
from jax.sharding import PartitionSpec as P


def from_root(array, axis, root):
    mine = lax.axis_index(axis) == root
    return lax.psum(jnp.where(mine, array, jnp.zeros_like(array)), axis)


def section_product(source_block, tile_set, row_slots, column_slots, live_count):
    tile_size = tile_set.shape[-1]
    tile_rows = source_block.shape[0] // tile_size
    feature_count = source_block.shape[1]
    column_rows = source_block.reshape(tile_rows, tile_size, feature_count)[column_slots]
    products = jnp.einsum("cuv,cvf->cuf", tile_set, column_rows, preferred_element_type=jnp.float32)
    slot_index = jnp.arange(tile_set.shape[0])
    live_flags = (slot_index < live_count).astype(jnp.float32)
    masked = products * live_flags[:, None, None]
    summed = jax.ops.segment_sum(masked, row_slots, num_segments=tile_rows)
    return summed.reshape(tile_rows * tile_size, feature_count)


def accumulate(sources, tile_sets, slot_lists, live_counts):
    summed_rows = jnp.zeros(sources[0].shape, jnp.float32)
    for step_index, source in enumerate(sources):
        summed_rows = summed_rows + section_product(
            source,
            tile_sets[step_index],
            slot_lists[step_index, 0],
            slot_lists[step_index, 1],
            live_counts[step_index],
        )
    return summed_rows


def body(
    features,
    weight,
    cotangent,
    node_order,
    forward_tiles,
    forward_slots,
    forward_count,
    backward_tiles,
    backward_slots,
    backward_count,
):
    rep_count = lax.axis_size("rep")
    row_count = lax.axis_size("rows")
    section_count = row_count // rep_count
    rep_index = lax.axis_index("rep")
    block_rows = features.shape[0]
    share_rows = block_rows // rep_count
    ordering = node_order[0]
    reordered = features[ordering]
    sources = [
        from_root(reordered, "rows", step_index * rep_count + rep_index)
        for step_index in range(section_count)
    ]
    partial_sum = accumulate(sources, forward_tiles[0, 0], forward_slots[0, 0], forward_count[0, 0])
    summed_rows = lax.psum(partial_sum, "rep")
    aggregated = summed_rows.astype(jnp.bfloat16)
    layer_output = jnp.dot(aggregated, weight, preferred_element_type=jnp.float32).astype(
        jnp.bfloat16
    )
    agg_share = lax.dynamic_slice_in_dim(aggregated, rep_index * share_rows, share_rows, 0)
    cot_share = lax.dynamic_slice_in_dim(cotangent, rep_index * share_rows, share_rows, 0)
    weight_term = lax.dot_general(
        agg_share, cot_share, (((0,), (0,)), ((), ())), preferred_element_type=jnp.float32
    )
    node_scale = 1.0 / math.sqrt(block_rows * row_count)
    grad_weight = lax.psum(weight_term, ("rows", "rep")) * node_scale
    back_rows = lax.dot_general(
        cotangent, weight, (((1,), (1,)), ((), ())), preferred_element_type=jnp.float32
    ).astype(jnp.bfloat16)
    back_sources = [
        from_root(back_rows, "rows", step_index * rep_count + rep_index)
        for step_index in range(section_count)
    ]
    partial_back = accumulate(
        back_sources, backward_tiles[0, 0], backward_slots[0, 0], backward_count[0, 0]
    )
    grad_reordered = lax.psum(partial_back, "rep").astype(jnp.bfloat16)
    unpermuted = jnp.zeros_like(grad_reordered).at[ordering].set(grad_reordered)
    grad_input = unpermuted * (features > 0).astype(jnp.bfloat16)
    return (layer_output, grad_weight, grad_input)


def solution(mesh):
    placed = (
        P("rows", None),
        P(),
        P("rows", None),
        P("rows", None),
        P("rows", "rep", None, None, None, None),
        P("rows", "rep", None, None, None),
        P("rows", "rep", None),
        P("rows", "rep", None, None, None, None),
        P("rows", "rep", None, None, None),
        P("rows", "rep", None),
    )
    return jax.shard_map(
        body,
        mesh=mesh,
        in_specs=placed,
        out_specs=(P("rows", None), P(), P("rows", None)),
        check_vma=False,
    )
```

profile of v0, /device:TPU:1, one launch (start us, length us, event | category | flops | bytes accessed | tf_op | source)
XLA Modules:
  0.0 817.3 jit_solution(15690195226813213871)
XLA Ops:
  8.0 4.6 gather_fusion
  22.4 299.8 %all-reduce.10.cloned.1.call-done = (bf16[8,128,256]{2,1,0:T(8,128)(2,1)}, bf16[8,128,256]{2,1,0:T(8,128)(2,1)}, bf16[8,128,256]{2,1,0:T(8,128)(2,1)}, bf16[8,12...) async-done(((bf16[8,128,256]{2,1,0:T(8,128)(2,1)}, ...) | async-done | bytes 4194320 | tf_op jit(solution)/shard_map/psum | solution.py:11
  328.1 5.7 copy.24
  338.6 5.7 copy.22
  349.1 5.6 copy.26
  359.5 5.6 copy.28
  365.3 6.5 scatter_fusion.1
  372.8 9.5 %scatter_fusion = f32[8,128,256]{2,1,0:T(8,128)} fusion(f32[8,128,256]{2,1,0:T(8,128)} %broadcast.185.clone, s32[32]{0:T(128)S(1)} %get-tuple-element.34, f32[32,128,256]{2,1,0:T(8,128)} %copy.22), kind=kCustom, calls=%fused_computation.9 | custom fusion | flops 1048576 | bytes 12583040 | tf_op jit(solution)/shard_map/scatter-add | solution.py:23
  383.7 6.5 scatter_fusion.2
  390.3 6.4 scatter_fusion.3
  397.9 63.4 %all-reduce.11 = bf16[1024,256]{1,0:T(8,128)(2,1)S(1)} all-reduce(f32[1024,256]{1,0:T(8,128)} %bitcast.140), channel_id=1, replica_groups=mesh['rows'=32,'rep'=8] {'rep'}, use_global_device_ids=true, to_apply=%region_8.9 | all-reduce | flops 262144 | bytes 1572864 | tf_op jit(solution)/shard_map/psum | solution.py:65
  466.3 4.3 multiply_bitcast_fusion.3
  470.5 4.2 multiply_bitcast_fusion.2
  484.4 5.6 copy.30
  490.1 5.6 copy.32
  495.7 5.6 copy.34
  501.3 5.7 copy.36
  507.1 6.5 scatter_fusion.4
  513.6 6.5 scatter_fusion.5
  520.3 6.5 scatter_fusion.6
  526.9 6.5 scatter_fusion.7
  536.7 184.0 %all-reduce.6.cloned.1.call-done = f32[256,256]{1,0:T(8,128)} async-done(((f32[256,256]{1,0:T(8,128)}), f32[256,256]{1,0:T(8,128)}) %all-reduce.6.cloned.1.call-update) | async-done | bytes 262160 | tf_op jit(solution)/shard_map/psum | solution.py:76
  722.4 82.0 %all-reduce.8.cloned.1.call-done = f32[1024,256]{1,0:T(8,128)} async-done(((f32[1024,256]{1,0:T(8,128)}), f32[1024,256]{1,0:T(8,128)}) %all-reduce.8.cloned.1.call-update) | async-done | bytes 1048592 | tf_op jit(solution)/shard_map/psum | solution.py:87
  804.3 5.5 scatter_custom_fusion.8
  (91 shorter events, 55.4 us)
Async XLA Ops:
  7.2 6.8 copy-start
  7.2 6.8 copy-start.11
  7.2 315.0 %all-reduce.10.cloned.1.call-start = ((), (), s32[]{:S(2)}) async-start(), calls=%async_computation.2 | async-start | bytes 8388608 | tf_op jit(solution)/shard_map/psum | solution.py:11
  14.0 1.8 copy-start.12
  14.0 5.0 copy-start.13
  14.0 8.2 %copy-start.14 = (s32[1,1,4,2,32]{4,3,2,1,0:T(2,128)S(1)}, s32[1,1,4,2,32]{4,3,2,1,0:T(2,128)}, u32[]{:S(2)}) copy-start(s32[1,1,4,2,32]{4,3,2,1,0:T(2,128)} %param.18) | copy-start | bytes 3076
  14.0 8.2 %copy-start.15 = (s32[1,1,4,2,32]{4,3,2,1,0:T(2,128)S(1)}, s32[1,1,4,2,32]{4,3,2,1,0:T(2,128)}, u32[]{:S(2)}) copy-start(s32[1,1,4,2,32]{4,3,2,1,0:T(2,128)} %param.15) | copy-start | bytes 3076
  15.7 705.0 %all-reduce.6.cloned.1.call-start = ((), (), s32[]{:S(2)}) async-start(), calls=%async_computation | async-start | bytes 524288 | tf_op jit(solution)/shard_map/psum | solution.py:76
  328.1 5.7 copy-start.8
  338.6 5.7 copy-start.7
  349.1 5.7 copy-start.6
  396.7 67.5 %copy-start.5 = (bf16[8,128,256]{2,1,0:T(8,128)(2,1)S(1)}, bf16[8,128,256]{2,1,0:T(8,128)(2,1)}, u32[]{:S(2)}) copy-start(bf16[8,128,256]{2,1,0:T(8,128)(2,1)} %get-tuple-element.8) | copy-start | bytes 1572868
  461.3 1.2 copy-start.10
  462.2 342.1 %all-reduce.8.cloned.1.call-start = ((), (), s32[]{:S(2)}) async-start(), calls=%async_computation.1 | async-start | bytes 2097152 | tf_op jit(solution)/shard_map/psum | solution.py:87
  466.3 4.3 copy-start.9
  470.5 4.2 copy-start.4
  475.4 4.2 copy-start.3
  526.8 283.9 %copy-start.1 = (bf16[1024,256]{1,0:T(8,128)(2,1)S(1)}, bf16[1024,256]{1,0:T(8,128)(2,1)}, u32[]{:S(2)}) copy-start(bf16[1024,256]{1,0:T(8,128)(2,1)} %param.12) | copy-start | bytes 1572868
  533.3 276.6 %copy-start.2 = (bf16[1024,256]{1,0:T(8,128)(2,1)S(1)}, bf16[1024,256]{1,0:T(8,128)(2,1)}, u32[]{:S(2)}) copy-start(bf16[1024,256]{1,0:T(8,128)(2,1)} %param.10) | copy-start | bytes 1572868
Sparse Core Ops, SparseCore 0:
  15.8 306.3 all-reduce.9
  462.4 258.2 all-reduce.5
  723.3 80.9 all-reduce.7
where the time goes:
time: 823 us; the launch traced here: 817 us
  waiting for transfers between devices  566 us (69%)
  other arithmetic  74 us (9%)
  blocking collectives  63.4 us (8%)
  local copies, waits for them, and re-layouts  61.5 us (7%)
  matrix products  38.1 us (5%)
  between operations  14.3 us (2%)
    psum x1, waiting for transfers between devices, from_root(): return lax.psum(jnp.where(mine, array, jnp.zeros_like(array)), axis)  300 us
    psum x1, waiting for transfers between devices, body(): grad_weight = lax.psum(weight_term, ('rows', 'rep')) * node_scale  184 us
    psum x1, waiting for transfers between devices, body(): grad_reordered = lax.psum(partial_back, 'rep').astype(jnp.bfloat16)  82 us
    psum x1, blocking collectives, body(): summed_rows = lax.psum(partial_sum, 'rep')  63.4 us
    scatter-add x8, other arithmetic, section_product(): summed = jax.ops.segment_sum(masked, row_slots, num_segments=tile_rows)  54.8 us
    mul x8, local copies, waits for them, and re-layouts, section_product(): masked = products * live_flags[:, None, None]  45.1 us
    dot_general x8, matrix products, section_product(): jnp.einsum('cuv,cvf->cuf', tile_set, column_rows, preferred_element_type=...  33.3 us
  transfers between devices with their start and end apart: 3, of which 3 were waited for; matrix products, arithmetic and copies ran while one was open for 10% of the time, Pallas kernels for 0%

commit v1 on v0

v1 whole, which is shorter than its diff:
```python
import math

import jax
import jax.numpy as jnp
from jax import lax
from jax.experimental import pallas as pl
from jax.experimental.pallas import tpu as pltpu
from jax.sharding import PartitionSpec as P

F32 = jnp.float32
BF16 = jnp.bfloat16
MESH = pl.DeviceIdType.MESH

N_X = 4
N_Y = 4
N_T = 4
N_REP = 8
BLOCK = 1024
FEAT = 256
TILE = 128
GRID = BLOCK // TILE
CAP = 32
CHUNK = 256
CHUNKS = BLOCK // CHUNK
SHARE = BLOCK // N_REP
GROWS = FEAT // N_REP


def rows_index(t, y, core):
    return (t * N_Y + y) * 2 + core


def layer_kernel(
    scale,
    map_ref,
    order_hbm,
    feat_hbm,
    weight_hbm,
    cot_hbm,
    ftiles_hbm,
    btiles_hbm,
    lo_ref,
    gw_ref,
    gi_ref,
    order_v,
    feat_v,
    weight_v,
    cot_v,
    ftiles_v,
    btiles_v,
    dense,
    unperm,
    src,
    part,
    part_b,
    rs_land,
    share_v,
    gterm,
    ga_land,
    gb_land,
    gc_land,
    gd_land,
    gfin,
    local_sem,
    chunk_recv,
    y_send,
    z_send,
    f_send,
    s_send,
    rs_send,
    rs_recv,
    ag_send,
    ag_recv,
    ga_send,
    ga_recv,
    gb_send,
    gb_recv,
    gc_send,
    gc_recv,
    gd_send,
    gd_recv,
    ge_send,
    ge_recv,
    out_sem,
):
    me = lax.axis_index("rows")
    rep = lax.axis_index("rep")
    core = me % 2
    y = (me // 2) % N_Y
    t = me // (2 * N_Y)
    x = rep // 2
    zl = rep % 2
    other = 1 - core
    t_up = (t + 1) % N_T
    t_dn = (t + N_T - 1) % N_T
    t_far = (t + 2) % N_T
    on_row = y == x
    source = jnp.logical_and(on_row, core == zl)
    not_source = jnp.logical_not(source)

    sibling = (rows_index(t, y, other), rep)
    up = (rows_index(t_up, y, core), rep)
    down = (rows_index(t_dn, y, core), rep)

    def y_peer(d, c):
        return (rows_index(t, (y + d) % N_Y, c), rep)

    def z_peer(d):
        return (rows_index((t + d) % N_T, y, core), rep)

    def rep_index(d):
        dx, dz = d // 2, d % 2
        px = (x + dx) % N_X
        pz = (zl + dz) % 2
        return px * 2 + pz

    def rep_from(d):
        dx, dz = d // 2, d % 2
        return ((x + N_X - dx) % N_X) * 2 + (zl + dz) % 2

    def rep_peer(d):
        return (me, rep_index(d))

    def remote(source_ref, target_ref, send, recv, device):
        return pltpu.make_async_remote_copy(
            src_ref=source_ref,
            dst_ref=target_ref,
            send_sem=send,
            recv_sem=recv,
            device_id=device,
            device_id_type=MESH,
        )

    loads = [
        pltpu.make_async_copy(order_hbm, order_v, local_sem.at[0]),
        pltpu.make_async_copy(feat_hbm, feat_v, local_sem.at[1]),
        pltpu.make_async_copy(weight_hbm, weight_v, local_sem.at[2]),
        pltpu.make_async_copy(cot_hbm, cot_v, local_sem.at[3]),
        pltpu.make_async_copy(ftiles_hbm, ftiles_v.at[:, pl.ds(0, CAP)], local_sem.at[4]),
        pltpu.make_async_copy(btiles_hbm, btiles_v.at[:, pl.ds(0, CAP)], local_sem.at[5]),
    ]
    tiles = (ftiles_v, btiles_v)
    for held in tiles:
        for s in range(N_T):
            held[s, CAP] = jnp.zeros((TILE, TILE), BF16)
    for load in loads:
        load.start()

    barrier = pltpu.get_barrier_semaphore()
    partners = [sibling]
    partners += [y_peer(d, core) for d in range(1, N_Y)]
    partners += [y_peer(d, other) for d in range(1, N_Y)]
    partners += [z_peer(d) for d in range(1, N_T)]
    partners += [rep_peer(d) for d in range(1, N_REP)]
    for partner in partners:
        pl.semaphore_signal(barrier, inc=1, device_id=partner, device_id_type=MESH)
    loads[0].wait()
    pl.semaphore_wait(barrier, len(partners))

    def chunk(p, block, q):
        return src.at[p, block, pl.ds(q * CHUNK, CHUNK), :]

    def chunk_to(p, block, q, send, device):
        ref = chunk(p, block, q)
        return remote(ref, ref, send, chunk_recv.at[p, block, q], device)

    def chunk_wait(p, block, q):
        chunk_to(p, block, q, s_send.at[0, 0, 0], sibling).wait_recv()

    def source_copies(p, q):
        c = q // (CHUNKS // 2)
        copies = [chunk_to(p, t, q, y_send.at[p, q, d], y_peer(d, c)) for d in range(1, N_Y)]
        copies.append(chunk_to(p, t, q, y_send.at[p, q, 0], sibling))
        return copies

    def own_copies(p, j):
        q = core * 2 + j
        return [
            chunk_to(p, t, q, z_send.at[p, j, 0], up),
            chunk_to(p, t, q, z_send.at[p, j, 1], down),
        ]

    def side_copy(p, block, j):
        return chunk_to(p, block, core * 2 + j, s_send.at[p, block, j], sibling)

    def forward_copy(p, j):
        if j == 0:
            return chunk_to(p, t_dn, core * 2, f_send.at[p, 0], up)
        return chunk_to(p, t_up, core * 2 + 1, f_send.at[p, 1], down)

    def spread_own(p):
        for j in range(2):

            @pl.when(not_source)
            def _():
                chunk_wait(p, t, core * 2 + j)

            for copy in own_copies(p, j):
                copy.start()

            @pl.when(jnp.logical_not(on_row))
            def _():
                side_copy(p, t, j).start()

    def spread_neighbours(p):
        for j in range(2):
            chunk_wait(p, t_dn, core * 2 + j)
            if j == 0:
                forward_copy(p, 0).start()
            side_copy(p, t_dn, j).start()
            chunk_wait(p, t_up, core * 2 + j)
            if j == 1:
                forward_copy(p, 1).start()
            side_copy(p, t_up, j).start()

    def spread_far(p):
        for j in range(2):
            chunk_wait(p, t_far, core * 2 + j)
            side_copy(p, t_far, j).start()

    def wait_side(p, block):
        for j in range(2):
            chunk_wait(p, block, other * 2 + j)

    def product(p, block, first=False):
        half = BLOCK // 2

        @pl.loop(0, 2)
        def _(m):
            rows = pl.ds(pl.multiple_of(m * half, half), half)
            term = jnp.dot(dense[p, block, rows, :], src[p, block], preferred_element_type=F32)
            if first:
                part[rows, :] = term
            else:
                part[rows, :] += term

    def lay_out(p):
        loads[4 + p].wait()

        @pl.loop(0, N_T * GRID)
        def _(step):
            s = step // GRID
            a = step % GRID
            rows = pl.ds(pl.multiple_of(a * TILE, TILE), TILE)
            for b in range(GRID):
                slot = map_ref[p, s, a * GRID + b]
                dense[p, s, rows, pl.ds(b * TILE, TILE)] = tiles[p][s, slot]

    @pl.when(source)
    def _():
        loads[1].wait()
        order_cols = jnp.transpose(jnp.broadcast_to(order_v[...], (TILE, BLOCK)))
        lanes = lax.broadcasted_iota(jnp.int32, (CHUNK, TILE), 1)
        for q in range(CHUNKS):
            wanted = order_cols[q * CHUNK : (q + 1) * CHUNK, :]
            one_hot = jnp.concatenate(
                [jnp.where(wanted == lanes + b * TILE, 1.0, 0.0).astype(BF16) for b in range(GRID)],
                axis=1,
            )
            picked = jnp.dot(one_hot, feat_v[...], preferred_element_type=F32)
            src[0, t, pl.ds(q * CHUNK, CHUNK), :] = picked.astype(BF16)
            for copy in source_copies(0, q):
                copy.start()

    @pl.when(not_source)
    def _():
        loads[1].wait()

    spread_own(0)
    loads[2].wait()
    loads[3].wait()

    @pl.when(source)
    def _():
        for q in range(CHUNKS):
            rows = pl.ds(q * CHUNK, CHUNK)
            back = lax.dot_general(
                cot_v[rows, :], weight_v[...], (((1,), (1,)), ((), ())), preferred_element_type=F32
            )
            src[1, t, rows, :] = back.astype(BF16)
            for copy in source_copies(1, q):
                copy.start()

    lay_out(0)

    def wait_rest(p):
        @pl.when(jnp.logical_not(source))
        def _():
            wait_side(p, t)

    wait_rest(0)
    product(0, t, first=True)
    spread_neighbours(0)
    spread_own(1)
    wait_side(0, t_dn)
    product(0, t_dn)
    wait_side(0, t_up)
    product(0, t_up)
    spread_far(0)
    wait_side(0, t_far)
    product(0, t_far)

    def share_rows(index):
        return pl.ds(pl.multiple_of(index * SHARE, SHARE), SHARE)

    def rs_copy(p, d):
        return remote(
            part_b.at[p, share_rows(rep_index(d)), :],
            rs_land.at[p, d],
            rs_send.at[p, d],
            rs_recv.at[p, d],
            rep_peer(d),
        )

    def ag_copy(p, out, d):
        return remote(
            share_v.at[p],
            out.at[share_rows(rep), :],
            ag_send.at[p, d],
            ag_recv.at[p, d],
            rep_peer(d),
        )

    def ag_wait(p, out, d):
        remote(
            share_v.at[p],
            out.at[share_rows(rep_from(d)), :],
            ag_send.at[p, d],
            ag_recv.at[p, d],
            rep_peer(d),
        ).wait_recv()

    part_b[0] = part[...].astype(BF16)
    for d in range(1, N_REP):
        rs_copy(0, d).start()

    lay_out(1)
    wait_rest(1)

    @pl.loop(0, GRID)
    def _(a):
        rows = pl.ds(pl.multiple_of(a * TILE, TILE), TILE)
        spots = lax.broadcasted_iota(jnp.int32, (TILE, BLOCK), 0) + a * TILE
        unperm[rows, :] = jnp.where(order_v[...] == spots, 1.0, 0.0).astype(BF16)

    def share_sum(p, own):
        total = own
        for d in range(1, N_REP):
            rs_copy(p, d).wait_recv()
            total = total + rs_land[p, d].astype(F32)
        return total

    total = share_sum(0, part[share_rows(rep), :])
    agg = total.astype(BF16)
    share_v[0] = jnp.dot(agg, weight_v[...], preferred_element_type=F32).astype(BF16)
    for d in range(1, N_REP):
        ag_copy(0, lo_ref, d).start()
    lo_own = pltpu.make_async_copy(share_v.at[0], lo_ref.at[share_rows(rep), :], out_sem.at[0])
    lo_own.start()

    gterm[...] = lax.dot_general(
        agg, cot_v[share_rows(rep), :], (((0,), (0,)), ((), ())), preferred_element_type=F32
    )

    def g_rows(index):
        return pl.ds(pl.multiple_of(index * GROWS, GROWS), GROWS)

    def ga_copy(d):
        return remote(
            gterm.at[g_rows(rep_index(d)), :],
            ga_land.at[d],
            ga_send.at[d],
            ga_recv.at[d],
            rep_peer(d),
        )

    for d in range(1, N_REP):
        ga_copy(d).start()

    product(1, t, first=True)
    spread_neighbours(1)
    wait_side(1, t_dn)
    product(1, t_dn)

    gsum = gterm[g_rows(rep), :]
    for d in range(1, N_REP):
        ga_copy(d).wait_recv()
        gsum = gsum + ga_land[d]

    def gb_copy(d):
        return remote(gb_land.at[y], gb_land.at[y], gb_send.at[d], gb_recv.at[d], y_peer(d, core))

    def gc_copy(d):
        return remote(gc_land.at[t], gc_land.at[t], gc_send.at[d], gc_recv.at[d], z_peer(d))

    def gd_copy():
        return remote(gd_land.at[core], gd_land.at[core], gd_send.at[0], gd_recv.at[0], sibling)

    def ge_copy(d):
        return remote(
            gfin, gw_ref.at[g_rows(rep), :], ge_send.at[d], ge_recv.at[d], rep_peer(d)
        )

    gb_land[y] = gsum
    for d in range(1, N_Y):
        gb_copy(d).start()

    wait_side(1, t_up)
    product(1, t_up)
    spread_far(1)

    for d in range(1, N_Y):
        gb_copy(d).wait_recv()
    gc_land[t] = gb_land[0] + gb_land[1] + gb_land[2] + gb_land[3]
    for d in range(1, N_T):
        gc_copy(d).start()

    wait_side(1, t_far)
    product(1, t_far)

    part_b[1] = part[...].astype(BF16)

    half = BLOCK // 2

    @pl.loop(0, 2)
    def _(m):
        rows = pl.ds(pl.multiple_of(m * half, half), half)
        part[rows, :] = jnp.dot(unperm[rows, :], part_b[1], preferred_element_type=F32)

    part_b[1] = part[...].astype(BF16)
    for d in range(1, N_REP):
        rs_copy(1, d).start()

    for d in range(1, N_T):
        gc_copy(d).wait_recv()
    gd_land[core] = gc_land[0] + gc_land[1] + gc_land[2] + gc_land[3]
    gd_copy().start()

    back_total = share_sum(1, part[share_rows(rep), :])
    keep = feat_v[share_rows(rep), :].astype(F32) > 0.0
    share_v[1] = jnp.where(keep, back_total, 0.0).astype(BF16)
    for d in range(1, N_REP):
        ag_copy(1, gi_ref, d).start()
    gi_own = pltpu.make_async_copy(share_v.at[1], gi_ref.at[share_rows(rep), :], out_sem.at[1])
    gi_own.start()

    gd_copy().wait_recv()
    gfin[...] = (gd_land[0] + gd_land[1]) * scale
    for d in range(1, N_REP):
        ge_copy(d).start()
    gw_own = pltpu.make_async_copy(gfin, gw_ref.at[g_rows(rep), :], out_sem.at[2])
    gw_own.start()

    for d in range(1, N_REP):
        ag_wait(0, lo_ref, d)
        ag_wait(1, gi_ref, d)
        ge_copy(d).wait_recv()
    lo_own.wait()
    gi_own.wait()
    gw_own.wait()

    for p in range(2):

        @pl.when(source)
        def _():
            for q in range(CHUNKS):
                for copy in source_copies(p, q):
                    copy.wait_send()

        for j in range(2):
            for copy in own_copies(p, j):
                copy.wait_send()
            forward_copy(p, j).wait_send()

            @pl.when(jnp.logical_not(on_row))
            def _():
                side_copy(p, t, j).wait_send()

            for block in (t_dn, t_up, t_far):
                side_copy(p, block, j).wait_send()
        for d in range(1, N_REP):
            rs_copy(p, d).wait_send()
            ag_copy(p, lo_ref, d).wait_send()
    for d in range(1, N_REP):
        ga_copy(d).wait_send()
        ge_copy(d).wait_send()
    for d in range(1, N_Y):
        gb_copy(d).wait_send()
    for d in range(1, N_T):
        gc_copy(d).wait_send()
    gd_copy().wait_send()


def slot_map(slots, count):
    index = jnp.arange(CAP, dtype=jnp.int32)
    key = slots[:, 0] * GRID + slots[:, 1]
    key = jnp.where(index[None, :] < count[:, None], key, -1)
    hit = key[:, :, None] == jnp.arange(GRID * GRID, dtype=jnp.int32)
    return jnp.min(jnp.where(hit, index[None, :, None], CAP), axis=1)


def body(
    features,
    weight,
    cotangent,
    node_order,
    forward_tiles,
    forward_slots,
    forward_count,
    backward_tiles,
    backward_slots,
    backward_count,
):
    maps = jnp.stack(
        [
            slot_map(forward_slots[0, 0], forward_count[0, 0]),
            slot_map(backward_slots[0, 0], backward_count[0, 0]),
        ]
    )
    scale = 1.0 / math.sqrt(BLOCK * lax.axis_size("rows"))
    any_spec = pl.BlockSpec(memory_space=pl.ANY)
    dma = pltpu.SemaphoreType.DMA

    def kernel(*refs):
        layer_kernel(scale, *refs)

    return pl.pallas_call(
        kernel,
        out_shape=[
            jax.ShapeDtypeStruct((BLOCK, FEAT), BF16),
            jax.ShapeDtypeStruct((FEAT, FEAT), F32),
            jax.ShapeDtypeStruct((BLOCK, FEAT), BF16),
        ],
        in_specs=[pl.BlockSpec(memory_space=pltpu.SMEM)] + [any_spec] * 6,
        out_specs=[any_spec] * 3,
        scratch_shapes=[
            pltpu.VMEM((1, BLOCK), jnp.int32),
            pltpu.VMEM((BLOCK, FEAT), BF16),
            pltpu.VMEM((FEAT, FEAT), BF16),
            pltpu.VMEM((BLOCK, FEAT), BF16),
            pltpu.VMEM((N_T, CAP + 1, TILE, TILE), BF16),
            pltpu.VMEM((N_T, CAP + 1, TILE, TILE), BF16),
            pltpu.VMEM((2, N_T, BLOCK, BLOCK), BF16),
            pltpu.VMEM((BLOCK, BLOCK), BF16),
            pltpu.VMEM((2, N_T, BLOCK, FEAT), BF16),
            pltpu.VMEM((BLOCK, FEAT), F32),
            pltpu.VMEM((2, BLOCK, FEAT), BF16),
            pltpu.VMEM((2, N_REP, SHARE, FEAT), BF16),
            pltpu.VMEM((2, SHARE, FEAT), BF16),
            pltpu.VMEM((FEAT, FEAT), F32),
            pltpu.VMEM((N_REP, GROWS, FEAT), F32),
            pltpu.VMEM((N_Y, GROWS, FEAT), F32),
            pltpu.VMEM((N_T, GROWS, FEAT), F32),
            pltpu.VMEM((2, GROWS, FEAT), F32),
            pltpu.VMEM((GROWS, FEAT), F32),
            dma((6,)),
            dma((2, N_T, CHUNKS)),
            dma((2, CHUNKS, N_Y)),
            dma((2, 2, 2)),
            dma((2, 2)),
            dma((2, N_T, 2)),
            dma((2, N_REP)),
            dma((2, N_REP)),
            dma((2, N_REP)),
            dma((2, N_REP)),
            dma((N_REP,)),
            dma((N_REP,)),
            dma((N_Y,)),
            dma((N_Y,)),
            dma((N_T,)),
            dma((N_T,)),
            dma((1,)),
            dma((1,)),
            dma((N_REP,)),
            dma((N_REP,)),
            dma((3,)),
        ],
        compiler_params=pltpu.CompilerParams(
            collective_id=0, has_side_effects=True, vmem_limit_bytes=56 * 1024 * 1024
        ),
    )(
        maps,
        node_order,
        features,
        weight,
        cotangent,
        forward_tiles[0, 0],
        backward_tiles[0, 0],
    )


def solution(mesh):
    placed = (
        P("rows", None),
        P(),
        P("rows", None),
        P("rows", None),
        P("rows", "rep", None, None, None, None),
        P("rows", "rep", None, None, None),
        P("rows", "rep", None),
        P("rows", "rep", None, None, None, None),
        P("rows", "rep", None, None, None),
        P("rows", "rep", None),
    )
    return jax.shard_map(
        body,
        mesh=mesh,
        in_specs=placed,
        out_specs=(P("rows", None), P(), P("rows", None)),
        check_vma=False,
    )
```

time: 823 us -> 106 us (0.13)
  waiting for transfers between devices: 566 us -> 0 us
  Pallas kernels: 0 us -> 95.5 us
  other arithmetic: 74 us -> 3.78 us
  blocking collectives: 63.4 us -> 0 us
  local copies, waits for them, and re-layouts: 61.5 us -> 5.4 us
  matrix products: 38.1 us -> 0 us
  between operations: 14.3 us -> 0.65 us
    psum x3 -> x0, waiting for transfers between devices: 566 us -> none  [the longest x1 300 us: from_root(): return lax.psum(jnp.where(mine, array, jnp.zeros_like(array)), axis)]
    pallas_call x0 -> x1, Pallas kernels: none -> 95.5 us  [body(): pl.pallas_call(kernel, out_shape=[jax.ShapeDtypeStruct((BLOCK, FEAT), BF1...]
    psum x1 -> x0, blocking collectives: 63.4 us -> none  [body(): summed_rows = lax.psum(partial_sum, 'rep')]
    scatter-add x8 -> x0, other arithmetic: 54.8 us -> none  [section_product(): summed = jax.ops.segment_sum(masked, row_slots, num_segments=tile_rows)]
    mul x8 -> x0, local copies, waits for them, and re-layouts: 45.1 us -> none  [section_product(): masked = products * live_flags[:, None, None]]
    dot_general x11 -> x0, matrix products: 38.1 us -> none  [the longest x8 33.3 us: section_product(): jnp.einsum('cuv,cvf->cuf', tile_set, column_rows, preferred_element_type=...]
    gather x9 -> x0, local copies, waits for them, and re-layouts: 13.4 us -> none  [the longest x8 8.85 us: section_product(): source_block.reshape(tile_rows, tile_size, feature_count)[column_slots]]
  transfers between devices with their start and end apart: 3 -> 0, of which waited for: 3 -> 0; matrix products, arithmetic and copies ran while one was open for 10% -> 0% of each run, Pallas kernels for 0% -> 0%
where the time goes in v1:
time: 106 us; the launch traced here: 105 us
  Pallas kernels  95.5 us (90%)
  local copies, waits for them, and re-layouts  5.4 us (5%)
  other arithmetic  3.78 us (4%)
    pallas_call x1, Pallas kernels, body(): pl.pallas_call(kernel, out_shape=[jax.ShapeDtypeStruct((BLOCK, FEAT), BF1...  95.5 us
    unnamed x3, local copies, waits for them, and re-layouts  5.4 us

profile of v1, /device:TPU:1, one launch (start us, length us, event | category | flops | bytes accessed | tf_op | source)
XLA Modules:
  0.0 105.3 jit_solution(914098344660867635)
XLA Ops:
  0.6 0.8 slice_add_fusion.1
  1.4 0.7 fusion
  2.1 0.1 select_reduce_fusion.1
  2.2 0.8 slice_add_fusion
  3.0 0.7 fusion.1
  3.7 0.1 select_reduce_fusion
  3.8 0.6 pad_add_fusion.refs_0_
  4.4 95.5 %shard_map.121 = (bf16[1024,256]{1,0:T(8,128)(2,1)}, f32[256,256]{1,0:T(8,128)}, bf16[1024,256]{1,0:T(8,128)(2,1)}) custom-call(s32[2,4,64]{2,1,0:T(4,128)} %pad_add_fusion.refs_0_, s32[1,1024]{1,0:T(1,128)} %refs_1_.1, bf16[1024,256]{1,0:T(8,128)(2,1)} %refs_2_.1, bf16[256,256]{1,0:T(8,128)(2,1)} %refs_3_.1, bf16[1024,256]{1,0:T(8,128)(2,1)} %refs_4_.1, ...), custom_call_target="tpu_custom_call" | custom-call | tf_op jit(solution)/shard_map/pallas_call | solution.py:527
  99.9 1.9 %copy.16 = bf16[1024,256]{1,0:T(8,128)(2,1)} copy(bf16[1024,256]{1,0:T(8,128)(2,1)} %get-tuple-element.6) | data formatting | bytes 1048576
  101.8 1.7 %copy.17 = f32[256,256]{1,0:T(8,128)} copy(f32[256,256]{1,0:T(8,128)} %get-tuple-element.7) | data formatting | bytes 524288
  103.5 1.9 %copy.18 = bf16[1024,256]{1,0:T(8,128)(2,1)} copy(bf16[1024,256]{1,0:T(8,128)(2,1)} %get-tuple-element.8) | data formatting | bytes 1048576

commit v2 on v1

v2 whole, which is shorter than its diff:
```python
import math

import jax
import jax.numpy as jnp
from jax import lax
from jax.experimental import pallas as pl
from jax.experimental.pallas import tpu as pltpu
from jax.sharding import PartitionSpec as P

F32 = jnp.float32
BF16 = jnp.bfloat16
MESH = pl.DeviceIdType.MESH

N_X = 4
N_Y = 4
N_T = 4
N_REP = 8
BLOCK = 1024
FEAT = 256
TILE = 128
GRID = BLOCK // TILE
CAP = 32
SHARE = BLOCK // N_REP
PART_A = 48
PART_B = SHARE - PART_A
GROWS = FEAT // 2 // N_REP


def rows_index(t, y, core):
    return (t * N_Y + y) * 2 + core


def layer_kernel(
    scale,
    fcount_ref,
    bcount_ref,
    fslots_hbm,
    bslots_hbm,
    order_hbm,
    feat_hbm,
    weight_hbm,
    cot_hbm,
    ftiles_hbm,
    btiles_hbm,
    lo_ref,
    gw_ref,
    gi_ref,
    slots_v,
    map_v,
    map_ref,
    order_v,
    feat_v,
    weight_v,
    cot_v,
    ftiles_v,
    btiles_v,
    dense,
    unperm,
    src,
    own,
    land_ya,
    land_xa,
    land_yb,
    part,
    part_b,
    rsx_land,
    rsz_land,
    rs_mid,
    rsz_out,
    rs_land,
    share_v,
    gterm,
    gd_land,
    gmid,
    ga_land,
    gb_land,
    gc_land,
    ghalf,
    local_sem,
    ya_send,
    ya_recv,
    xa_send,
    xa_recv,
    za_send,
    za_recv,
    zb_send,
    zb_recv,
    yb_send,
    yb_recv,
    xb_send,
    xb_recv,
    side_send,
    side_recv,
    rsx_send,
    rsx_recv,
    rsz_send,
    rsz_recv,
    agz_send,
    rs_send,
    rs_recv,
    ag_send,
    ag_recv,
    ga_send,
    ga_recv,
    gb_send,
    gb_recv,
    gc_send,
    gc_recv,
    gd_send,
    gd_recv,
    ge_send,
    ge_recv,
    gf_send,
    gf_recv,
    out_sem,
):
    me = lax.axis_index("rows")
    rep = lax.axis_index("rep")
    core = me % 2
    y = (me // 2) % N_Y
    t = me // (2 * N_Y)
    x = rep // 2
    zl = rep % 2
    other = 1 - core
    straight = core == zl
    crossed = jnp.logical_not(straight)
    blocks = [(t + d) % N_T for d in (0, 1, 3, 2)]

    sibling = (rows_index(t, y, other), rep)

    def y_peer(d):
        return (rows_index(t, (y + d) % N_Y, core), rep)

    def cross_peer(d):
        return (rows_index((t + d) % N_T, y, zl), x * 2 + core)

    def z_peer(d):
        return (rows_index((t + d) % N_T, y, core), rep)

    def rep_index(d):
        dx, dz = d // 2, d % 2
        px = (x + dx) % N_X
        pz = (zl + dz) % 2
        return px * 2 + pz

    def rep_from(d):
        dx, dz = d // 2, d % 2
        return ((x + N_X - dx) % N_X) * 2 + (zl + dz) % 2

    def rep_peer(d):
        return (me, rep_index(d))

    def remote(source_ref, target_ref, send, recv, device):
        return pltpu.make_async_remote_copy(
            src_ref=source_ref,
            dst_ref=target_ref,
            send_sem=send,
            recv_sem=recv,
            device_id=device,
            device_id_type=MESH,
        )

    loads = [
        pltpu.make_async_copy(order_hbm, order_v, local_sem.at[0]),
        pltpu.make_async_copy(feat_hbm, feat_v, local_sem.at[1]),
        pltpu.make_async_copy(weight_hbm, weight_v, local_sem.at[2]),
        pltpu.make_async_copy(cot_hbm, cot_v, local_sem.at[3]),
        pltpu.make_async_copy(ftiles_hbm, ftiles_v.at[:, pl.ds(0, CAP)], local_sem.at[4]),
        pltpu.make_async_copy(btiles_hbm, btiles_v.at[:, pl.ds(0, CAP)], local_sem.at[5]),
        pltpu.make_async_copy(fslots_hbm, slots_v.at[0], local_sem.at[6]),
        pltpu.make_async_copy(bslots_hbm, slots_v.at[1], local_sem.at[7]),
    ]
    tiles = (ftiles_v, btiles_v)
    for held in tiles:
        for s in range(N_T):
            held[s, CAP] = jnp.zeros((TILE, TILE), BF16)
    for load in loads:
        load.start()

    barrier = pltpu.get_barrier_semaphore()
    partners = [sibling]
    partners += [y_peer(d) for d in range(1, N_Y)]
    partners += [z_peer(d) for d in range(1, N_T)]
    partners += [cross_peer(d) for d in range(1, N_T)]
    partners += [rep_peer(d) for d in range(1, N_REP)]
    for partner in partners:
        pl.semaphore_signal(barrier, inc=1, device_id=partner, device_id_type=MESH)

    @pl.when(crossed)
    def _():
        pl.semaphore_signal(barrier, inc=1, device_id=cross_peer(0), device_id_type=MESH)

    def share_rows(index):
        return pl.ds(pl.multiple_of(index * SHARE, SHARE), SHARE)

    loads[0].wait()
    wanted = jnp.transpose(jnp.broadcast_to(order_v[0:1, share_rows(rep)], (SHARE, SHARE)))
    lanes = lax.broadcasted_iota(jnp.int32, (SHARE, TILE), 1)
    one_hot = jnp.concatenate(
        [jnp.where(wanted == lanes + b * TILE, 1.0, 0.0).astype(BF16) for b in range(GRID)], axis=1
    )
    loads[1].wait()
    own[0] = jnp.dot(one_hot, feat_v[...], preferred_element_type=F32).astype(BF16)
    land_ya[0, y] = own[0, 0:PART_A, :]

    @pl.when(straight)
    def _():
        land_yb[0, y, t] = own[0, PART_A:SHARE, :]
        pl.semaphore_wait(barrier, len(partners))

    @pl.when(crossed)
    def _():
        pl.semaphore_wait(barrier, len(partners) + 1)

    first_a = pl.ds(0, PART_A)
    last_b = pl.ds(PART_A, PART_B)

    def ya_copy(p, d):
        ref = land_ya.at[p, y]
        return remote(ref, ref, ya_send.at[p, d], ya_recv.at[p, d], y_peer(d))

    def xa_copy(p, d):
        return remote(
            land_ya.at[p, (x + d) % N_X], land_xa.at[p, x], xa_send.at[p, d], xa_recv.at[p, d], rep_peer(2 * d)
        )

    def za_copy(p, d):
        return remote(
            land_xa.at[p],
            src.at[p, t, :, zl, first_a, :],
            za_send.at[p, d],
            za_recv.at[p, d],
            cross_peer(d),
        )

    def zb_copy(p, d):
        return remote(
            own.at[p, last_b, :], land_yb.at[p, y, t], zb_send.at[p, d], zb_recv.at[p, d], cross_peer(d)
        )

    def yb_copy(p, i, d):
        ref = land_yb.at[p, y, blocks[i]]
        return remote(ref, ref, yb_send.at[p, i, d], yb_recv.at[p, i, d], y_peer(d))

    def xb_copy(p, i, d):
        return remote(
            land_yb.at[p, (x + d) % N_X, blocks[i]],
            src.at[p, blocks[i], x, core, last_b, :],
            xb_send.at[p, i, d],
            xb_recv.at[p, i, d],
            rep_peer(2 * d),
        )

    def side_copy(p, i):
        ref = src.at[p, blocks[i], :, core]
        return remote(ref, ref, side_send.at[p, i], side_recv.at[p, i], sibling)

    from_z = (0, 3, 1, 2)

    def begin(p):
        for d in (2, 1, 3):
            zb_copy(p, d).start()

        @pl.when(crossed)
        def _():
            zb_copy(p, 0).start()

        for d in (2, 1, 3):
            ya_copy(p, d).start()

    def z_wait(copy, i):
        if i == 0:

            @pl.when(crossed)
            def _():
                copy.wait_recv()

        else:
            copy.wait_recv()

    def a_over_x(p):
        for d in (1, 2, 3):
            ya_copy(p, d).wait_recv()
        for d in (2, 1, 3):
            xa_copy(p, d).start()
        land_xa[p, x] = land_ya[p, x]

    def a_over_z(p):
        for d in (1, 2, 3):
            xa_copy(p, d).wait_recv()
        for d in (2, 1, 3):
            za_copy(p, d).start()

        @pl.when(crossed)
        def _():
            za_copy(p, 0).start()

        @pl.when(straight)
        def _():
            src[p, t, :, zl, first_a, :] = land_xa[p]

    def b_over_y(p):
        for i in range(N_T):
            z_wait(zb_copy(p, from_z[i]), i)
            for d in (2, 1, 3):
                yb_copy(p, i, d).start()

    def b_over_x(p):
        for i in range(N_T):
            for d in (1, 2, 3):
                yb_copy(p, i, d).wait_recv()
            for d in (2, 1, 3):
                xb_copy(p, i, d).start()
            src[p, blocks[i], x, core, last_b, :] = land_yb[p, x, blocks[i]]

    def finish(p, i):
        for d in (1, 2, 3):
            xb_copy(p, i, d).wait_recv()
        z_wait(za_copy(p, from_z[i]), i)
        side_copy(p, i).start()

    def use(p, i):
        side_copy(p, i).wait_recv()
        product(p, blocks[i], first=i == 0)

    def product(p, block, first=False):
        half = BLOCK // 2

        @pl.loop(0, 2)
        def _(m):
            rows = pl.ds(pl.multiple_of(m * half, half), half)
            term = jnp.dot(
                dense[p, block, rows, :], src[p, block].reshape(BLOCK, FEAT), preferred_element_type=F32
            )
            if first:
                part[rows, :] = term
            else:
                part[rows, :] += term

    def slot_maps():
        loads[6].wait()
        loads[7].wait()
        count_refs = (fcount_ref, bcount_ref)
        rows8 = lax.broadcasted_iota(jnp.int32, (2 * N_T, 1), 0)
        live = jnp.zeros((2 * N_T, 1), jnp.int32)
        for row in range(2 * N_T):
            live = jnp.where(rows8 == row, count_refs[row // N_T][row % N_T], live)
        keys = jnp.concatenate(
            [slots_v[p, s, 0:1, :] * GRID + slots_v[p, s, 1:2, :] for p in range(2) for s in range(N_T)],
            axis=0,
        )
        cells = lax.broadcasted_iota(jnp.int32, (2 * N_T, TILE), 1)
        found = jnp.full((2 * N_T, TILE), CAP, jnp.int32)
        for slot in range(CAP):
            hit = jnp.logical_and(keys[:, slot : slot + 1] == cells, live > slot)
            found = jnp.where(hit, slot, found)
        map_v[...] = found
        to_scalar = pltpu.make_async_copy(map_v, map_ref, local_sem.at[8])
        to_scalar.start()
        to_scalar.wait()

    def lay_out(p):
        loads[4 + p].wait()

        @pl.loop(0, N_T * GRID)
        def _(step):
            s = step // GRID
            a = step % GRID
            rows = pl.ds(pl.multiple_of(a * TILE, TILE), TILE)
            for b in range(GRID):
                slot = map_ref[p * N_T + s, a * GRID + b]
                dense[p, s, rows, pl.ds(b * TILE, TILE)] = tiles[p][s, slot]

    begin(0)
    loads[2].wait()
    loads[3].wait()
    own[1] = lax.dot_general(
        cot_v[share_rows(rep), :], weight_v[...], (((1,), (1,)), ((), ())), preferred_element_type=F32
    ).astype(BF16)
    land_ya[1, y] = own[1, 0:PART_A, :]

    @pl.when(straight)
    def _():
        land_yb[1, y, t] = own[1, PART_A:SHARE, :]

    slot_maps()
    a_over_x(0)
    b_over_y(0)
    a_over_z(0)
    lay_out(0)
    b_over_x(0)
    begin(1)
    finish(0, 0)
    finish(0, 1)
    use(0, 0)
    a_over_x(1)
    finish(0, 2)
    use(0, 1)
    finish(0, 3)
    b_over_y(1)
    use(0, 2)
    a_over_z(1)
    use(0, 3)

    def pair_rows(index):
        return pl.ds(pl.multiple_of(index * 2 * SHARE, 2 * SHARE), 2 * SHARE)

    def rsx_copy(d):
        return remote(
            part_b.at[0, pair_rows((x + d) % N_X), :],
            rsx_land.at[d],
            rsx_send.at[d],
            rsx_recv.at[d],
            rep_peer(2 * d),
        )

    def rsz_copy():
        return remote(rsz_out, rsz_land, rsz_send.at[0], rsz_recv.at[0], rep_peer(1))

    part_b[0] = part[...].astype(BF16)
    for d in (2, 1, 3):
        rsx_copy(d).start()

    lay_out(1)

    @pl.loop(0, GRID)
    def _(a):
        rows = pl.ds(pl.multiple_of(a * TILE, TILE), TILE)
        spots = lax.broadcasted_iota(jnp.int32, (TILE, BLOCK), 0) + a * TILE
        unperm[rows, :] = jnp.where(order_v[...] == spots, 1.0, 0.0).astype(BF16)

    total = part[pair_rows(x), :]
    for d in range(1, N_X):
        rsx_copy(d).wait_recv()
        total = total + rsx_land[d].astype(F32)
    rs_mid[...] = total
    rsz_out[...] = rs_mid[share_rows(1 - zl), :].astype(BF16)
    rsz_copy().start()

    b_over_x(1)
    finish(1, 0)

    partner = rep_index(1)

    def ag_own(d):
        return remote(
            share_v.at[0], lo_ref.at[share_rows(rep), :], ag_send.at[0, d], ag_recv.at[0, d], rep_peer(d)
        )

    def ag_pass(d):
        rows = share_rows(partner)
        return remote(
            lo_ref.at[rows, :], lo_ref.at[rows, :], agz_send.at[d], ag_recv.at[0, 2 * d + 1], rep_peer(2 * d)
        )

    rsz_copy().wait_recv()
    agg = (rs_mid[share_rows(zl), :] + rsz_land[...].astype(F32)).astype(BF16)
    share_v[0] = jnp.dot(agg, weight_v[...], preferred_element_type=F32).astype(BF16)
    for d in (1, 4, 2, 6):
        ag_own(d).start()
    lo_own = pltpu.make_async_copy(share_v.at[0], lo_ref.at[share_rows(rep), :], out_sem.at[0])
    lo_own.start()

    gterm[...] = lax.dot_general(
        agg, cot_v[share_rows(rep), :], (((0,), (0,)), ((), ())), preferred_element_type=F32
    )
    ghalf_rows = FEAT // 2

    def core_rows(index):
        return pl.ds(pl.multiple_of(index * ghalf_rows, ghalf_rows), ghalf_rows)

    def gd_copy():
        return remote(
            gterm.at[core_rows(other), :], gd_land, gd_send.at[0], gd_recv.at[0], sibling
        )

    def g_rows(index):
        return pl.ds(pl.multiple_of(index * GROWS, GROWS), GROWS)

    def ga_copy(d):
        return remote(
            gmid.at[g_rows(rep_index(d)), :],
            ga_land.at[d],
            ga_send.at[d],
            ga_recv.at[d],
            rep_peer(d),
        )

    def gb_copy(d):
        return remote(gb_land.at[y], gb_land.at[y], gb_send.at[d], gb_recv.at[d], y_peer(d))

    def gc_copy(d):
        return remote(gc_land.at[t], gc_land.at[t], gc_send.at[d], gc_recv.at[d], z_peer(d))

    def ge_copy(d):
        mine = ghalf.at[g_rows(rep), :]
        return remote(mine, mine, ge_send.at[d], ge_recv.at[d], rep_peer(d))

    def gf_copy():
        return remote(
            ghalf, gw_ref.at[core_rows(core), :], gf_send.at[0], gf_recv.at[0], sibling
        )

    gd_copy().start()

    use(1, 0)
    finish(1, 1)

    ag_own(1).wait_recv()
    for d in range(1, N_X):
        ag_pass(d).start()
    gd_copy().wait_recv()
    gmid[...] = gterm[core_rows(core), :] + gd_land[...]
    for d in range(1, N_REP):
        ga_copy(d).start()

    use(1, 1)
    finish(1, 2)
    finish(1, 3)

    gsum = gmid[g_rows(rep), :]
    for d in range(1, N_REP):
        ga_copy(d).wait_recv()
        gsum = gsum + ga_land[d]
    gb_land[y] = gsum
    for d in range(1, N_Y):
        gb_copy(d).start()

    use(1, 2)
    use(1, 3)
    part_b[1] = part[...].astype(BF16)
    half = BLOCK // 2

    @pl.loop(0, 2)
    def _(m):
        rows = pl.ds(pl.multiple_of(m * half, half), half)
        part[rows, :] = jnp.dot(unperm[rows, :], part_b[1], preferred_element_type=F32)

    part_b[1] = part[...].astype(BF16)

    def rs_copy(d):
        return remote(
            part_b.at[1, share_rows(rep_index(d)), :],
            rs_land.at[d],
            rs_send.at[d],
            rs_recv.at[d],
            rep_peer(d),
        )

    def ag_copy(d):
        return remote(
            share_v.at[1], gi_ref.at[share_rows(rep), :], ag_send.at[1, d], ag_recv.at[1, d], rep_peer(d)
        )

    far_first = (5, 4, 3, 7, 2, 6, 1)
    for d in far_first:
        rs_copy(d).start()

    for d in range(1, N_Y):
        gb_copy(d).wait_recv()
    gc_land[t] = gb_land[0] + gb_land[1] + gb_land[2] + gb_land[3]
    for d in range(1, N_T):
        gc_copy(d).start()

    back_total = part[share_rows(rep), :]
    for d in range(1, N_REP):
        rs_copy(d).wait_recv()
        back_total = back_total + rs_land[d].astype(F32)
    keep = feat_v[share_rows(rep), :].astype(F32) > 0.0
    share_v[1] = jnp.where(keep, back_total, 0.0).astype(BF16)
    for d in far_first:
        ag_copy(d).start()
    gi_own = pltpu.make_async_copy(share_v.at[1], gi_ref.at[share_rows(rep), :], out_sem.at[1])
    gi_own.start()

    for d in range(1, N_T):
        gc_copy(d).wait_recv()
    ghalf[g_rows(rep), :] = (gc_land[0] + gc_land[1] + gc_land[2] + gc_land[3]) * scale
    for d in range(1, N_REP):
        ge_copy(d).start()
    for d in range(1, N_REP):
        ge_copy(d).wait_recv()
    gf_copy().start()
    gw_own = pltpu.make_async_copy(ghalf, gw_ref.at[core_rows(core), :], out_sem.at[2])
    gw_own.start()

    for d in (2, 4, 6, 3, 5, 7):
        ag_own(d).wait_recv()
    for d in range(1, N_REP):
        ag_copy(d).wait_recv()
    gf_copy().wait_recv()
    lo_own.wait()
    gi_own.wait()
    gw_own.wait()

    for p in range(2):

        @pl.when(crossed)
        def _():
            zb_copy(p, 0).wait_send()
            za_copy(p, 0).wait_send()

        for d in (1, 2, 3):
            ya_copy(p, d).wait_send()
            xa_copy(p, d).wait_send()
            za_copy(p, d).wait_send()
            zb_copy(p, d).wait_send()
            for i in range(N_T):
                yb_copy(p, i, d).wait_send()
                xb_copy(p, i, d).wait_send()
        for i in range(N_T):
            side_copy(p, i).wait_send()
    for d in (1, 2, 4, 6):
        ag_own(d).wait_send()
    for d in range(1, N_X):
        rsx_copy(d).wait_send()
        ag_pass(d).wait_send()
    rsz_copy().wait_send()
    for d in range(1, N_REP):
        rs_copy(d).wait_send()
        ag_copy(d).wait_send()
        ga_copy(d).wait_send()
        ge_copy(d).wait_send()
    for d in range(1, N_Y):
        gb_copy(d).wait_send()
    for d in range(1, N_T):
        gc_copy(d).wait_send()
    gd_copy().wait_send()
    gf_copy().wait_send()


def copy_kernel(*refs):
    count = len(refs) // 2
    for i in range(count):
        refs[count + i][...] = refs[i][...]


def body(
    features,
    weight,
    cotangent,
    node_order,
    forward_tiles,
    forward_slots,
    forward_count,
    backward_tiles,
    backward_slots,
    backward_count,
):
    scale = 1.0 / math.sqrt(BLOCK * lax.axis_size("rows"))
    any_spec = pl.BlockSpec(memory_space=pl.ANY)
    dma = pltpu.SemaphoreType.DMA

    def kernel(*refs):
        layer_kernel(scale, *refs)

    results = pl.pallas_call(
        kernel,
        out_shape=[
            jax.ShapeDtypeStruct((BLOCK, FEAT), BF16),
            jax.ShapeDtypeStruct((FEAT, FEAT), F32),
            jax.ShapeDtypeStruct((BLOCK, FEAT), BF16),
        ],
        in_specs=[pl.BlockSpec(memory_space=pltpu.SMEM)] * 2 + [any_spec] * 8,
        out_specs=[any_spec] * 3,
        scratch_shapes=[
            pltpu.VMEM((2, N_T, 2, CAP), jnp.int32),
            pltpu.VMEM((2 * N_T, TILE), jnp.int32),
            pltpu.SMEM((2 * N_T, TILE), jnp.int32),
            pltpu.VMEM((1, BLOCK), jnp.int32),
            pltpu.VMEM((BLOCK, FEAT), BF16),
            pltpu.VMEM((FEAT, FEAT), BF16),
            pltpu.VMEM((BLOCK, FEAT), BF16),
            pltpu.VMEM((N_T, CAP + 1, TILE, TILE), BF16),
            pltpu.VMEM((N_T, CAP + 1, TILE, TILE), BF16),
            pltpu.VMEM((2, N_T, BLOCK, BLOCK), BF16),
            pltpu.VMEM((BLOCK, BLOCK), BF16),
            pltpu.VMEM((2, N_T, N_X, 2, SHARE, FEAT), BF16),
            pltpu.VMEM((2, SHARE, FEAT), BF16),
            pltpu.VMEM((2, N_Y, PART_A, FEAT), BF16),
            pltpu.VMEM((2, N_X, PART_A, FEAT), BF16),
            pltpu.VMEM((2, N_Y, N_T, PART_B, FEAT), BF16),
            pltpu.VMEM((BLOCK, FEAT), F32),
            pltpu.VMEM((2, BLOCK, FEAT), BF16),
            pltpu.VMEM((N_X, 2 * SHARE, FEAT), BF16),
            pltpu.VMEM((SHARE, FEAT), BF16),
            pltpu.VMEM((2 * SHARE, FEAT), F32),
            pltpu.VMEM((SHARE, FEAT), BF16),
            pltpu.VMEM((N_REP, SHARE, FEAT), BF16),
            pltpu.VMEM((2, SHARE, FEAT), BF16),
            pltpu.VMEM((FEAT, FEAT), F32),
            pltpu.VMEM((FEAT // 2, FEAT), F32),
            pltpu.VMEM((FEAT // 2, FEAT), F32),
            pltpu.VMEM((N_REP, GROWS, FEAT), F32),
            pltpu.VMEM((N_Y, GROWS, FEAT), F32),
            pltpu.VMEM((N_T, GROWS, FEAT), F32),
            pltpu.VMEM((FEAT // 2, FEAT), F32),
            dma((9,)),
            dma((2, N_Y)),
            dma((2, N_Y)),
            dma((2, N_Y)),
            dma((2, N_Y)),
            dma((2, N_Y)),
            dma((2, N_Y)),
            dma((2, N_Y)),
            dma((2, N_Y)),
            dma((2, N_T, N_Y)),
            dma((2, N_T, N_Y)),
            dma((2, N_T, N_Y)),
            dma((2, N_T, N_Y)),
            dma((2, N_T)),
            dma((2, N_T)),
            dma((N_X,)),
            dma((N_X,)),
            dma((1,)),
            dma((1,)),
            dma((N_X,)),
            dma((N_REP,)),
            dma((N_REP,)),
            dma((2, N_REP)),
            dma((2, N_REP)),
            dma((N_REP,)),
            dma((N_REP,)),
            dma((N_Y,)),
            dma((N_Y,)),
            dma((N_T,)),
            dma((N_T,)),
            dma((1,)),
            dma((1,)),
            dma((N_REP,)),
            dma((N_REP,)),
            dma((1,)),
            dma((1,)),
            dma((3,)),
        ],
        compiler_params=pltpu.CompilerParams(
            collective_id=0, has_side_effects=True, vmem_limit_bytes=56 * 1024 * 1024
        ),
    )(
        forward_count[0, 0],
        backward_count[0, 0],
        forward_slots[0, 0],
        backward_slots[0, 0],
        node_order,
        features,
        weight,
        cotangent,
        forward_tiles[0, 0],
        backward_tiles[0, 0],
    )
    return pl.pallas_call(
        copy_kernel,
        out_shape=[jax.ShapeDtypeStruct(r.shape, r.dtype) for r in results],
        in_specs=[pl.BlockSpec(memory_space=pltpu.VMEM)] * 3,
        out_specs=[pl.BlockSpec(memory_space=pltpu.VMEM)] * 3,
    )(*results)


def solution(mesh):
    placed = (
        P("rows", None),
        P(),
        P("rows", None),
        P("rows", None),
        P("rows", "rep", None, None, None, None),
        P("rows", "rep", None, None, None),
        P("rows", "rep", None),
        P("rows", "rep", None, None, None, None),
        P("rows", "rep", None, None, None),
        P("rows", "rep", None),
    )
    return jax.shard_map(
        body,
        mesh=mesh,
        in_specs=placed,
        out_specs=(P("rows", None), P(), P("rows", None)),
        check_vma=False,
    )
```

time: 106 us -> 85.8 us (0.81)
  Pallas kernels: 95.5 us -> 85 us
  local copies, waits for them, and re-layouts: 5.4 us -> 0 us
  other arithmetic: 3.78 us -> 0 us
    pallas_call x1, Pallas kernels: 95.5 us -> 82.7 us  [body(): pl.pallas_call(kernel, out_shape=[jax.ShapeDtypeStruct((BLOCK, FEAT), BF1...]
    unnamed x3 -> x0, local copies, waits for them, and re-layouts: 5.4 us -> none
    pallas_call x0 -> x1, Pallas kernels: none -> 2.35 us  [body(): pl.pallas_call(copy_kernel, out_shape=[jax.ShapeDtypeStruct(r.shape, r.dt...]
    add x2 -> x0, other arithmetic: 1.54 us -> none  [slot_map(): key = slots[:, 0] * GRID + slots[:, 1]]
    select_n x2 -> x0, other arithmetic: 1.45 us -> none  [slot_map(): key = jnp.where(index[None, :] < count[:, None], key, -1)]
where the time goes in v2:
time: 85.8 us; the launch traced here: 85.7 us
  Pallas kernels  85 us (99%)
    pallas_call x1, Pallas kernels, body(): pl.pallas_call(kernel, out_shape=[jax.ShapeDtypeStruct((BLOCK, FEAT), BF1...  82.7 us
    pallas_call x1, Pallas kernels, body(): pl.pallas_call(copy_kernel, out_shape=[jax.ShapeDtypeStruct(r.shape, r.dt...  2.35 us

profile of v2, /device:TPU:1, one launch (start us, length us, event | category | flops | bytes accessed | tf_op | source)
XLA Modules:
  0.0 85.7 jit_solution(4891394391417374748)
XLA Ops:
  0.6 82.7 %shard_map.121 = (bf16[1024,256]{1,0:T(8,128)(2,1)}, f32[256,256]{1,0:T(8,128)}, bf16[1024,256]{1,0:T(8,128)(2,1)}) custom-call(s32[4]{0:T(128)} %bitcast.10, s32[4]{0:T(128)} %bitcast.11, s32[4,2,32]{2,1,0:T(2,128)} %bitcast.8, s32[4,2,32]{2,1,0:T(2,128)} %bitcast.9, s32[1,1024]{1,0:T(1,128)} %refs_4_.1, bf16[1024,256]{1,0:T(8,128)(2,1)} %refs_5_.1, ...), custom_call_target="tpu_custom_call" | custom-call | tf_op jit(solution)/shard_map/pallas_call | solution.py:657
  83.3 2.4 %shard_map.122 = (bf16[1024,256]{1,0:T(8,128)(2,1)}, f32[256,256]{1,0:T(8,128)}, bf16[1024,256]{1,0:T(8,128)(2,1)}) custom-call(bf16[1024,256]{1,0:T(8,128)(2,1)} %get-tuple-element.6.refs_0_, f32[256,256]{1,0:T(8,128)} %get-tuple-element.7.refs_1_, bf16[1024,256]{1,0:T(8,128)(2,1)} %get-tuple-element.8.refs_2_), custom_call_target="tpu_custom_call" | custom-call | tf_op jit(solution)/shard_map/pallas_call | solution.py:751

commit v3 on v2

--- a/solution.py
+++ b/solution.py
@@ -21,8 +21,8 @@
 GRID = BLOCK // TILE
 CAP = 32
 SHARE = BLOCK // N_REP
-PART_A = 48
-PART_B = SHARE - PART_A
+PART_A = (48, 48)
+PART_B = tuple(SHARE - rows for rows in PART_A)
 GROWS = FEAT // 2 // N_REP
 
 
@@ -58,9 +58,12 @@
     unperm,
     src,
     own,
-    land_ya,
-    land_xa,
-    land_yb,
+    ya_f,
+    ya_b,
+    xa_f,
+    xa_b,
+    yb_f,
+    yb_b,
     part,
     part_b,
     rsx_land,
@@ -201,33 +204,36 @@
     )
     loads[1].wait()
     own[0] = jnp.dot(one_hot, feat_v[...], preferred_element_type=F32).astype(BF16)
-    land_ya[0, y] = own[0, 0:PART_A, :]
+    ya_f[y] = own[0, 0 : PART_A[0], :]
 
     @pl.when(straight)
     def _():
-        land_yb[0, y, t] = own[0, PART_A:SHARE, :]
+        yb_f[y, t] = own[0, PART_A[0] : SHARE, :]
         pl.semaphore_wait(barrier, len(partners))
 
     @pl.when(crossed)
     def _():
         pl.semaphore_wait(barrier, len(partners) + 1)
 
-    first_a = pl.ds(0, PART_A)
-    last_b = pl.ds(PART_A, PART_B)
+    land_ya = (ya_f, ya_b)
+    land_xa = (xa_f, xa_b)
+    land_yb = (yb_f, yb_b)
+    first_a = [pl.ds(0, rows) for rows in PART_A]
+    last_b = [pl.ds(rows, SHARE - rows) for rows in PART_A]
 
     def ya_copy(p, d):
-        ref = land_ya.at[p, y]
+        ref = land_ya[p].at[y]
         return remote(ref, ref, ya_send.at[p, d], ya_recv.at[p, d], y_peer(d))
 
     def xa_copy(p, d):
         return remote(
-            land_ya.at[p, (x + d) % N_X], land_xa.at[p, x], xa_send.at[p, d], xa_recv.at[p, d], rep_peer(2 * d)
+            land_ya[p].at[(x + d) % N_X], land_xa[p].at[x], xa_send.at[p, d], xa_recv.at[p, d], rep_peer(2 * d)
         )
 
     def za_copy(p, d):
         return remote(
-            land_xa.at[p],
-            src.at[p, t, :, zl, first_a, :],
+            land_xa[p],
+            src.at[p, t, :, zl, first_a[p], :],
             za_send.at[p, d],
             za_recv.at[p, d],
             cross_peer(d),
@@ -235,17 +241,17 @@
 
     def zb_copy(p, d):
         return remote(
-            own.at[p, last_b, :], land_yb.at[p, y, t], zb_send.at[p, d], zb_recv.at[p, d], cross_peer(d)
+            own.at[p, last_b[p], :], land_yb[p].at[y, t], zb_send.at[p, d], zb_recv.at[p, d], cross_peer(d)
         )
 
     def yb_copy(p, i, d):
-        ref = land_yb.at[p, y, blocks[i]]
+        ref = land_yb[p].at[y, blocks[i]]
         return remote(ref, ref, yb_send.at[p, i, d], yb_recv.at[p, i, d], y_peer(d))
 
     def xb_copy(p, i, d):
         return remote(
-            land_yb.at[p, (x + d) % N_X, blocks[i]],
-            src.at[p, blocks[i], x, core, last_b, :],
+            land_yb[p].at[(x + d) % N_X, blocks[i]],
+            src.at[p, blocks[i], x, core, last_b[p], :],
             xb_send.at[p, i, d],
             xb_recv.at[p, i, d],
             rep_peer(2 * d),
@@ -283,7 +289,7 @@
             ya_copy(p, d).wait_recv()
         for d in (2, 1, 3):
             xa_copy(p, d).start()
-        land_xa[p, x] = land_ya[p, x]
+        land_xa[p][x] = land_ya[p][x]
 
     def a_over_z(p):
         for d in (1, 2, 3):
@@ -297,7 +303,7 @@
 
         @pl.when(straight)
         def _():
-            src[p, t, :, zl, first_a, :] = land_xa[p]
+            src[p, t, :, zl, first_a[p], :] = land_xa[p][...]
 
     def b_over_y(p):
         for i in range(N_T):
@@ -311,7 +317,7 @@
                 yb_copy(p, i, d).wait_recv()
             for d in (2, 1, 3):
                 xb_copy(p, i, d).start()
-            src[p, blocks[i], x, core, last_b, :] = land_yb[p, x, blocks[i]]
+            src[p, blocks[i], x, core, last_b[p], :] = land_yb[p][x, blocks[i]]
 
     def finish(p, i):
         for d in (1, 2, 3):
@@ -319,23 +325,17 @@
         z_wait(za_copy(p, from_z[i]), i)
         side_copy(p, i).start()
 
-    def use(p, i):
-        side_copy(p, i).wait_recv()
-        product(p, blocks[i], first=i == 0)
-
-    def product(p, block, first=False):
-        half = BLOCK // 2
-
-        @pl.loop(0, 2)
-        def _(m):
-            rows = pl.ds(pl.multiple_of(m * half, half), half)
-            term = jnp.dot(
-                dense[p, block, rows, :], src[p, block].reshape(BLOCK, FEAT), preferred_element_type=F32
+    def use_all(p):
+        part[...] = jnp.zeros((BLOCK, FEAT), F32)
+
+        @pl.loop(0, N_T)
+        def _(i):
+            block = (t + i + i // 2 * (5 - 2 * i)) % N_T
+            ref = src.at[p, block, :, core]
+            remote(ref, ref, side_send.at[p, i], side_recv.at[p, i], sibling).wait_recv()
+            part[...] += jnp.dot(
+                dense[p, block], src[p, block].reshape(BLOCK, FEAT), preferred_element_type=F32
             )
-            if first:
-                part[rows, :] = term
-            else:
-                part[rows, :] += term
 
     def slot_maps():
         loads[6].wait()
@@ -377,30 +377,35 @@
     own[1] = lax.dot_general(
         cot_v[share_rows(rep), :], weight_v[...], (((1,), (1,)), ((), ())), preferred_element_type=F32
     ).astype(BF16)
-    land_ya[1, y] = own[1, 0:PART_A, :]
+    ya_b[y] = own[1, 0 : PART_A[1], :]
 
     @pl.when(straight)
     def _():
-        land_yb[1, y, t] = own[1, PART_A:SHARE, :]
-
+        yb_b[y, t] = own[1, PART_A[1] : SHARE, :]
+
+    begin(1)
     slot_maps()
     a_over_x(0)
     b_over_y(0)
     a_over_z(0)
     lay_out(0)
     b_over_x(0)
-    begin(1)
+    lay_out(1)
+
+    @pl.loop(0, GRID)
+    def _(a):
+        rows = pl.ds(pl.multiple_of(a * TILE, TILE), TILE)
+        spots = lax.broadcasted_iota(jnp.int32, (TILE, BLOCK), 0) + a * TILE
+        unperm[rows, :] = jnp.where(order_v[...] == spots, 1.0, 0.0).astype(BF16)
+
     finish(0, 0)
     finish(0, 1)
-    use(0, 0)
     a_over_x(1)
     finish(0, 2)
-    use(0, 1)
     finish(0, 3)
     b_over_y(1)
-    use(0, 2)
     a_over_z(1)
-    use(0, 3)
+    use_all(0)
 
     def pair_rows(index):
         return pl.ds(pl.multiple_of(index * 2 * SHARE, 2 * SHARE), 2 * SHARE)
@@ -421,14 +426,7 @@
     for d in (2, 1, 3):
         rsx_copy(d).start()
 
-    lay_out(1)
-
-    @pl.loop(0, GRID)
-    def _(a):
-        rows = pl.ds(pl.multiple_of(a * TILE, TILE), TILE)
-        spots = lax.broadcasted_iota(jnp.int32, (TILE, BLOCK), 0) + a * TILE
-        unperm[rows, :] = jnp.where(order_v[...] == spots, 1.0, 0.0).astype(BF16)
-
+    b_over_x(1)
     total = part[pair_rows(x), :]
     for d in range(1, N_X):
         rsx_copy(d).wait_recv()
@@ -437,8 +435,8 @@
     rsz_out[...] = rs_mid[share_rows(1 - zl), :].astype(BF16)
     rsz_copy().start()
 
-    b_over_x(1)
     finish(1, 0)
+    finish(1, 1)
 
     partner = rep_index(1)
 
@@ -503,20 +501,39 @@
 
     gd_copy().start()
 
-    use(1, 0)
-    finish(1, 1)
-
-    ag_own(1).wait_recv()
-    for d in range(1, N_X):
-        ag_pass(d).start()
+    finish(1, 2)
+    finish(1, 3)
     gd_copy().wait_recv()
     gmid[...] = gterm[core_rows(core), :] + gd_land[...]
     for d in range(1, N_REP):
         ga_copy(d).start()
 
-    use(1, 1)
-    finish(1, 2)
-    finish(1, 3)
+    use_all(1)
+    part_b[1] = part[...].astype(BF16)
+    part[...] = jnp.dot(unperm[...], part_b[1], preferred_element_type=F32)
+    part_b[1] = part[...].astype(BF16)
+
+    def rs_copy(d):
+        return remote(
+            part_b.at[1, share_rows(rep_index(d)), :],
+            rs_land.at[d],
+            rs_send.at[d],
+            rs_recv.at[d],
+            rep_peer(d),
+        )
+
+    def ag_copy(d):
+        return remote(
+            share_v.at[1], gi_ref.at[share_rows(rep), :], ag_send.at[1, d], ag_recv.at[1, d], rep_peer(d)
+        )
+
+    far_first = (5, 4, 3, 7, 2, 6, 1)
+    for d in far_first:
+        rs_copy(d).start()
+
+    ag_own(1).wait_recv()
+    for d in range(1, N_X):
+        ag_pass(d).start()
 
     gsum = gmid[g_rows(rep), :]
     for d in range(1, N_REP):
@@ -525,42 +542,16 @@
     gb_land[y] = gsum
     for d in range(1, N_Y):
         gb_copy(d).start()
-
-    use(1, 2)
-    use(1, 3)
-    part_b[1] = part[...].astype(BF16)
-    half = BLOCK // 2
-
-    @pl.loop(0, 2)
-    def _(m):
-        rows = pl.ds(pl.multiple_of(m * half, half), half)
-        part[rows, :] = jnp.dot(unperm[rows, :], part_b[1], preferred_element_type=F32)
-
-    part_b[1] = part[...].astype(BF16)
-
-    def rs_copy(d):
-        return remote(
-            part_b.at[1, share_rows(rep_index(d)), :],
-            rs_land.at[d],
-            rs_send.at[d],
-            rs_recv.at[d],
-            rep_peer(d),
-        )
-
-    def ag_copy(d):
-        return remote(
-            share_v.at[1], gi_ref.at[share_rows(rep), :], ag_send.at[1, d], ag_recv.at[1, d], rep_peer(d)
-        )
-
-    far_first = (5, 4, 3, 7, 2, 6, 1)
-    for d in far_first:
-        rs_copy(d).start()
-
     for d in range(1, N_Y):
         gb_copy(d).wait_recv()
     gc_land[t] = gb_land[0] + gb_land[1] + gb_land[2] + gb_land[3]
     for d in range(1, N_T):
         gc_copy(d).start()
+    for d in range(1, N_T):
+        gc_copy(d).wait_recv()
+    ghalf[g_rows(rep), :] = (gc_land[0] + gc_land[1] + gc_land[2] + gc_land[3]) * scale
+    for d in range(1, N_REP):
+        ge_copy(d).start()
 
     back_total = part[share_rows(rep), :]
     for d in range(1, N_REP):
@@ -573,25 +564,11 @@
     gi_own = pltpu.make_async_copy(share_v.at[1], gi_ref.at[share_rows(rep), :], out_sem.at[1])
     gi_own.start()
 
-    for d in range(1, N_T):
-        gc_copy(d).wait_recv()
-    ghalf[g_rows(rep), :] = (gc_land[0] + gc_land[1] + gc_land[2] + gc_land[3]) * scale
-    for d in range(1, N_REP):
-        ge_copy(d).start()
     for d in range(1, N_REP):
         ge_copy(d).wait_recv()
     gf_copy().start()
     gw_own = pltpu.make_async_copy(ghalf, gw_ref.at[core_rows(core), :], out_sem.at[2])
     gw_own.start()
-
-    for d in (2, 4, 6, 3, 5, 7):
-        ag_own(d).wait_recv()
-    for d in range(1, N_REP):
-        ag_copy(d).wait_recv()
-    gf_copy().wait_recv()
-    lo_own.wait()
-    gi_own.wait()
-    gw_own.wait()
 
     for p in range(2):
 
@@ -618,16 +595,25 @@
     rsz_copy().wait_send()
     for d in range(1, N_REP):
         rs_copy(d).wait_send()
-        ag_copy(d).wait_send()
         ga_copy(d).wait_send()
-        ge_copy(d).wait_send()
     for d in range(1, N_Y):
         gb_copy(d).wait_send()
     for d in range(1, N_T):
         gc_copy(d).wait_send()
     gd_copy().wait_send()
+
+    for d in (2, 4, 6, 3, 5, 7):
+        ag_own(d).wait_recv()
+    for d in range(1, N_REP):
+        ag_copy(d).wait_recv()
+    gf_copy().wait_recv()
+    lo_own.wait()
+    gi_own.wait()
+    gw_own.wait()
+    for d in range(1, N_REP):
+        ag_copy(d).wait_send()
+        ge_copy(d).wait_send()
     gf_copy().wait_send()
-
 
 def copy_kernel(*refs):
     count = len(refs) // 2
@@ -677,9 +663,12 @@
             pltpu.VMEM((BLOCK, BLOCK), BF16),
             pltpu.VMEM((2, N_T, N_X, 2, SHARE, FEAT), BF16),
             pltpu.VMEM((2, SHARE, FEAT), BF16),
-            pltpu.VMEM((2, N_Y, PART_A, FEAT), BF16),
-            pltpu.VMEM((2, N_X, PART_A, FEAT), BF16),
-            pltpu.VMEM((2, N_Y, N_T, PART_B, FEAT), BF16),
+            pltpu.VMEM((N_Y, PART_A[0], FEAT), BF16),
+            pltpu.VMEM((N_Y, PART_A[1], FEAT), BF16),
+            pltpu.VMEM((N_X, PART_A[0], FEAT), BF16),
+            pltpu.VMEM((N_X, PART_A[1], FEAT), BF16),
+            pltpu.VMEM((N_Y, N_T, PART_B[0], FEAT), BF16),
+            pltpu.VMEM((N_Y, N_T, PART_B[1], FEAT), BF16),
             pltpu.VMEM((BLOCK, FEAT), F32),
             pltpu.VMEM((2, BLOCK, FEAT), BF16),
             pltpu.VMEM((N_X, 2 * SHARE, FEAT), BF16),

time: 85.8 us -> 77.6 us (0.904)
  Pallas kernels: 85 us -> 76.8 us
    pallas_call x1, Pallas kernels: 82.7 us -> 74.4 us  [body(): pl.pallas_call(kernel, out_shape=[jax.ShapeDtypeStruct((BLOCK, FEAT), BF1...]
where the time goes in v3:
time: 77.6 us; the launch traced here: 77.4 us
  Pallas kernels  76.8 us (99%)
    pallas_call x1, Pallas kernels, body(): pl.pallas_call(kernel, out_shape=[jax.ShapeDtypeStruct((BLOCK, FEAT), BF1...  74.4 us
    pallas_call x1, Pallas kernels, body(): pl.pallas_call(copy_kernel, out_shape=[jax.ShapeDtypeStruct(r.shape, r.dt...  2.35 us

profile of v3, /device:TPU:1, one launch (start us, length us, event | category | flops | bytes accessed | tf_op | source)
XLA Modules:
  0.0 77.4 jit_solution(11142263760050931377)
XLA Ops:
  0.6 74.4 %shard_map.121 = (bf16[1024,256]{1,0:T(8,128)(2,1)}, f32[256,256]{1,0:T(8,128)}, bf16[1024,256]{1,0:T(8,128)(2,1)}) custom-call(s32[4]{0:T(128)} %bitcast.10, s32[4]{0:T(128)} %bitcast.11, s32[4,2,32]{2,1,0:T(2,128)} %bitcast.8, s32[4,2,32]{2,1,0:T(2,128)} %bitcast.9, s32[1,1024]{1,0:T(1,128)} %refs_4_.1, bf16[1024,256]{1,0:T(8,128)(2,1)} %refs_5_.1, ...), custom_call_target="tpu_custom_call" | custom-call | tf_op jit(solution)/shard_map/pallas_call | solution.py:643
  75.1 2.4 %shard_map.122 = (bf16[1024,256]{1,0:T(8,128)(2,1)}, f32[256,256]{1,0:T(8,128)}, bf16[1024,256]{1,0:T(8,128)(2,1)}) custom-call(bf16[1024,256]{1,0:T(8,128)(2,1)} %get-tuple-element.6.refs_0_, f32[256,256]{1,0:T(8,128)} %get-tuple-element.7.refs_1_, bf16[1024,256]{1,0:T(8,128)(2,1)} %get-tuple-element.8.refs_2_), custom_call_target="tpu_custom_call" | custom-call | tf_op jit(solution)/shard_map/pallas_call | solution.py:740

commit v4 on v3

--- a/solution.py
+++ b/solution.py
@@ -21,6 +21,7 @@
 GRID = BLOCK // TILE
 CAP = 32
 SHARE = BLOCK // N_REP
+PIECES = 2
 PART_A = (48, 48)
 PART_B = tuple(SHARE - rows for rows in PART_A)
 GROWS = FEAT // 2 // N_REP
@@ -119,36 +120,36 @@
 ):
     me = lax.axis_index("rows")
     rep = lax.axis_index("rep")
-    core = me % 2
-    y = (me // 2) % N_Y
-    t = me // (2 * N_Y)
-    x = rep // 2
-    zl = rep % 2
+    core = lax.rem(me, 2)
+    y = lax.rem(lax.div(me, 2), N_Y)
+    t = lax.div(me, 2 * N_Y)
+    x = lax.div(rep, 2)
+    zl = lax.rem(rep, 2)
     other = 1 - core
     straight = core == zl
     crossed = jnp.logical_not(straight)
-    blocks = [(t + d) % N_T for d in (0, 1, 3, 2)]
+    blocks = [lax.rem(t + d, N_T) for d in (0, 1, 3, 2)]
 
     sibling = (rows_index(t, y, other), rep)
 
     def y_peer(d):
-        return (rows_index(t, (y + d) % N_Y, core), rep)
+        return (rows_index(t, lax.rem(y + d, N_Y), core), rep)
 
     def cross_peer(d):
-        return (rows_index((t + d) % N_T, y, zl), x * 2 + core)
+        return (rows_index(lax.rem(t + d, N_T), y, zl), x * 2 + core)
 
     def z_peer(d):
-        return (rows_index((t + d) % N_T, y, core), rep)
+        return (rows_index(lax.rem(t + d, N_T), y, core), rep)
 
     def rep_index(d):
         dx, dz = d // 2, d % 2
-        px = (x + dx) % N_X
-        pz = (zl + dz) % 2
+        px = lax.rem(x + dx, N_X)
+        pz = lax.rem(zl + dz, 2)
         return px * 2 + pz
 
     def rep_from(d):
         dx, dz = d // 2, d % 2
-        return ((x + N_X - dx) % N_X) * 2 + (zl + dz) % 2
+        return (lax.rem(x + N_X - dx, N_X)) * 2 + lax.rem(zl + dz, 2)
 
     def rep_peer(d):
         return (me, rep_index(d))
@@ -177,7 +178,7 @@
     for held in tiles:
         for s in range(N_T):
             held[s, CAP] = jnp.zeros((TILE, TILE), BF16)
-    for load in loads:
+    for load in loads[:4] + loads[6:]:
         load.start()
 
     barrier = pltpu.get_barrier_semaphore()
@@ -227,7 +228,7 @@
 
     def xa_copy(p, d):
         return remote(
-            land_ya[p].at[(x + d) % N_X], land_xa[p].at[x], xa_send.at[p, d], xa_recv.at[p, d], rep_peer(2 * d)
+            land_ya[p].at[lax.rem(x + d, N_X)], land_xa[p].at[x], xa_send.at[p, d], xa_recv.at[p, d], rep_peer(2 * d)
         )
 
     def za_copy(p, d):
@@ -250,7 +251,7 @@
 
     def xb_copy(p, i, d):
         return remote(
-            land_yb[p].at[(x + d) % N_X, blocks[i]],
+            land_yb[p].at[lax.rem(x + d, N_X), blocks[i]],
             src.at[p, blocks[i], x, core, last_b[p], :],
             xb_send.at[p, i, d],
             xb_recv.at[p, i, d],
@@ -330,7 +331,7 @@
 
         @pl.loop(0, N_T)
         def _(i):
-            block = (t + i + i // 2 * (5 - 2 * i)) % N_T
+            block = lax.rem(t + i + i // 2 * (5 - 2 * i), N_T)
             ref = src.at[p, block, :, core]
             remote(ref, ref, side_send.at[p, i], side_recv.at[p, i], sibling).wait_recv()
             part[...] += jnp.dot(
@@ -372,6 +373,8 @@
                 dense[p, s, rows, pl.ds(b * TILE, TILE)] = tiles[p][s, slot]
 
     begin(0)
+    loads[4].start()
+    loads[5].start()
     loads[2].wait()
     loads[3].wait()
     own[1] = lax.dot_general(
@@ -412,7 +415,7 @@
 
     def rsx_copy(d):
         return remote(
-            part_b.at[0, pair_rows((x + d) % N_X), :],
+            part_b.at[0, pair_rows(lax.rem(x + d, N_X)), :],
             rsx_land.at[d],
             rsx_send.at[d],
             rsx_recv.at[d],
@@ -513,23 +516,33 @@
     part[...] = jnp.dot(unperm[...], part_b[1], preferred_element_type=F32)
     part_b[1] = part[...].astype(BF16)
 
-    def rs_copy(d):
-        return remote(
-            part_b.at[1, share_rows(rep_index(d)), :],
-            rs_land.at[d],
-            rs_send.at[d],
-            rs_recv.at[d],
+    piece = SHARE // PIECES
+
+    def piece_rows(index, h):
+        return pl.ds(pl.multiple_of(index * SHARE + h * piece, piece), piece)
+
+    def rs_copy(d, h):
+        return remote(
+            part_b.at[1, piece_rows(rep_index(d), h), :],
+            rs_land.at[d, pl.ds(h * piece, piece)],
+            rs_send.at[h, d],
+            rs_recv.at[h, d],
             rep_peer(d),
         )
 
-    def ag_copy(d):
-        return remote(
-            share_v.at[1], gi_ref.at[share_rows(rep), :], ag_send.at[1, d], ag_recv.at[1, d], rep_peer(d)
+    def ag_copy(d, h):
+        return remote(
+            share_v.at[1, pl.ds(h * piece, piece)],
+            gi_ref.at[piece_rows(rep, h), :],
+            ag_send.at[1 + h, d],
+            ag_recv.at[1 + h, d],
+            rep_peer(d),
         )
 
     far_first = (5, 4, 3, 7, 2, 6, 1)
-    for d in far_first:
-        rs_copy(d).start()
+    for h in range(PIECES):
+        for d in far_first:
+            rs_copy(d, h).start()
 
     ag_own(1).wait_recv()
     for d in range(1, N_X):
@@ -553,14 +566,15 @@
     for d in range(1, N_REP):
         ge_copy(d).start()
 
-    back_total = part[share_rows(rep), :]
-    for d in range(1, N_REP):
-        rs_copy(d).wait_recv()
-        back_total = back_total + rs_land[d].astype(F32)
-    keep = feat_v[share_rows(rep), :].astype(F32) > 0.0
-    share_v[1] = jnp.where(keep, back_total, 0.0).astype(BF16)
-    for d in far_first:
-        ag_copy(d).start()
+    for h in range(PIECES):
+        back_total = part[piece_rows(rep, h), :]
+        for d in range(1, N_REP):
+            rs_copy(d, h).wait_recv()
+            back_total = back_total + rs_land[d, h * piece : (h + 1) * piece].astype(F32)
+        keep = feat_v[piece_rows(rep, h), :].astype(F32) > 0.0
+        share_v[1, h * piece : (h + 1) * piece] = jnp.where(keep, back_total, 0.0).astype(BF16)
+        for d in far_first:
+            ag_copy(d, h).start()
     gi_own = pltpu.make_async_copy(share_v.at[1], gi_ref.at[share_rows(rep), :], out_sem.at[1])
     gi_own.start()
 
@@ -594,7 +608,8 @@
         ag_pass(d).wait_send()
     rsz_copy().wait_send()
     for d in range(1, N_REP):
-        rs_copy(d).wait_send()
+        for h in range(PIECES):
+            rs_copy(d, h).wait_send()
         ga_copy(d).wait_send()
     for d in range(1, N_Y):
         gb_copy(d).wait_send()
@@ -605,20 +620,34 @@
     for d in (2, 4, 6, 3, 5, 7):
         ag_own(d).wait_recv()
     for d in range(1, N_REP):
-        ag_copy(d).wait_recv()
+        for h in range(PIECES):
+            ag_copy(d, h).wait_recv()
     gf_copy().wait_recv()
     lo_own.wait()
     gi_own.wait()
     gw_own.wait()
     for d in range(1, N_REP):
-        ag_copy(d).wait_send()
+        for h in range(PIECES):
+            ag_copy(d, h).wait_send()
         ge_copy(d).wait_send()
     gf_copy().wait_send()
 
 def copy_kernel(*refs):
-    count = len(refs) // 2
-    for i in range(count):
-        refs[count + i][...] = refs[i][...]
+    sources, targets, held, sems = refs[:3], refs[3:6], refs[6:9], refs[9]
+    pieces = []
+    for n in range(3):
+        rows = sources[n].shape[0] // 4
+        for c in range(4):
+            part = pl.ds(c * rows, rows)
+            sem = sems.at[n * 4 + c]
+            inward = pltpu.make_async_copy(sources[n].at[part], held[n].at[part], sem)
+            inward.start()
+            pieces.append((inward, pltpu.make_async_copy(held[n].at[part], targets[n].at[part], sem)))
+    for inward, outward in pieces:
+        inward.wait()
+        outward.start()
+    for _, outward in pieces:
+        outward.wait()
 
 
 def body(
@@ -704,10 +733,10 @@
             dma((1,)),
             dma((1,)),
             dma((N_X,)),
-            dma((N_REP,)),
-            dma((N_REP,)),
-            dma((2, N_REP)),
-            dma((2, N_REP)),
+            dma((PIECES, N_REP)),
+            dma((PIECES, N_REP)),
+            dma((1 + PIECES, N_REP)),
+            dma((1 + PIECES, N_REP)),
             dma((N_REP,)),
             dma((N_REP,)),
             dma((N_Y,)),
@@ -740,8 +769,10 @@
     return pl.pallas_call(
         copy_kernel,
         out_shape=[jax.ShapeDtypeStruct(r.shape, r.dtype) for r in results],
-        in_specs=[pl.BlockSpec(memory_space=pltpu.VMEM)] * 3,
-        out_specs=[pl.BlockSpec(memory_space=pltpu.VMEM)] * 3,
+        in_specs=[any_spec] * 3,
+        out_specs=[any_spec] * 3,
+        scratch_shapes=[pltpu.VMEM(r.shape, r.dtype) for r in results] + [dma((12,))],
+        compiler_params=pltpu.CompilerParams(vmem_limit_bytes=56 * 1024 * 1024),
     )(*results)
 
 

time: 77.6 us -> 76.8 us (0.990)
  Pallas kernels: 76.8 us -> 76 us
where the time goes in v4:
time: 76.8 us; the launch traced here: 76.7 us
  Pallas kernels  76 us (99%)
    pallas_call x1, Pallas kernels, body(): pl.pallas_call(kernel, out_shape=[jax.ShapeDtypeStruct((BLOCK, FEAT), BF1...  73.9 us
    pallas_call x1, Pallas kernels, body(): pl.pallas_call(copy_kernel, out_shape=[jax.ShapeDtypeStruct(r.shape, r.dt...  2.13 us

profile of v4, /device:TPU:1, one launch (start us, length us, event | category | flops | bytes accessed | tf_op | source)
XLA Modules:
  0.0 76.7 jit_solution(17872270000929429143)
XLA Ops:
  0.6 73.9 %shard_map.121 = (bf16[1024,256]{1,0:T(8,128)(2,1)}, f32[256,256]{1,0:T(8,128)}, bf16[1024,256]{1,0:T(8,128)(2,1)}) custom-call(s32[4]{0:T(128)} %bitcast.10, s32[4]{0:T(128)} %bitcast.11, s32[4,2,32]{2,1,0:T(2,128)} %bitcast.8, s32[4,2,32]{2,1,0:T(2,128)} %bitcast.9, s32[1,1024]{1,0:T(1,128)} %refs_4_.1, bf16[1024,256]{1,0:T(8,128)(2,1)} %refs_5_.1, ...), custom_call_target="tpu_custom_call" | custom-call | tf_op jit(solution)/shard_map/pallas_call | solution.py:672
  74.5 2.1 %shard_map.122 = (bf16[1024,256]{1,0:T(8,128)(2,1)}, f32[256,256]{1,0:T(8,128)}, bf16[1024,256]{1,0:T(8,128)(2,1)}) custom-call(bf16[1024,256]{1,0:T(8,128)(2,1)} %get-tuple-element.6.refs_0_, f32[256,256]{1,0:T(8,128)} %get-tuple-element.7.refs_1_, bf16[1024,256]{1,0:T(8,128)(2,1)} %get-tuple-element.8.refs_2_), custom_call_target="tpu_custom_call" | custom-call | tf_op jit(solution)/shard_map/pallas_call | solution.py:769

commit v5 on v4

--- a/solution.py
+++ b/solution.py
@@ -395,12 +395,6 @@
     b_over_x(0)
     lay_out(1)
 
-    @pl.loop(0, GRID)
-    def _(a):
-        rows = pl.ds(pl.multiple_of(a * TILE, TILE), TILE)
-        spots = lax.broadcasted_iota(jnp.int32, (TILE, BLOCK), 0) + a * TILE
-        unperm[rows, :] = jnp.where(order_v[...] == spots, 1.0, 0.0).astype(BF16)
-
     finish(0, 0)
     finish(0, 1)
     a_over_x(1)
@@ -430,6 +424,13 @@
         rsx_copy(d).start()
 
     b_over_x(1)
+
+    @pl.loop(0, GRID)
+    def _(a):
+        rows = pl.ds(pl.multiple_of(a * TILE, TILE), TILE)
+        spots = lax.broadcasted_iota(jnp.int32, (TILE, BLOCK), 0) + a * TILE
+        unperm[rows, :] = jnp.where(order_v[...] == spots, 1.0, 0.0).astype(BF16)
+
     total = part[pair_rows(x), :]
     for d in range(1, N_X):
         rsx_copy(d).wait_recv()

time: 76.8 us -> 76.6 us (level)
  no operation moved by 1% of the time
where the time goes in v5:
time: 76.6 us; the launch traced here: 76.4 us
  Pallas kernels  75.8 us (99%)
    pallas_call x1, Pallas kernels, body(): pl.pallas_call(kernel, out_shape=[jax.ShapeDtypeStruct((BLOCK, FEAT), BF1...  73.6 us
    pallas_call x1, Pallas kernels, body(): pl.pallas_call(copy_kernel, out_shape=[jax.ShapeDtypeStruct(r.shape, r.dt...  2.13 us

profile of v5, /device:TPU:1, one launch (start us, length us, event | category | flops | bytes accessed | tf_op | source)
XLA Modules:
  0.0 76.4 jit_solution(2698471765931394907)
XLA Ops:
  0.6 73.6 %shard_map.121 = (bf16[1024,256]{1,0:T(8,128)(2,1)}, f32[256,256]{1,0:T(8,128)}, bf16[1024,256]{1,0:T(8,128)(2,1)}) custom-call(s32[4]{0:T(128)} %bitcast.10, s32[4]{0:T(128)} %bitcast.11, s32[4,2,32]{2,1,0:T(2,128)} %bitcast.8, s32[4,2,32]{2,1,0:T(2,128)} %bitcast.9, s32[1,1024]{1,0:T(1,128)} %refs_4_.1, bf16[1024,256]{1,0:T(8,128)(2,1)} %refs_5_.1, ...), custom_call_target="tpu_custom_call" | custom-call | tf_op jit(solution)/shard_map/pallas_call | solution.py:673
  74.3 2.1 %shard_map.122 = (bf16[1024,256]{1,0:T(8,128)(2,1)}, f32[256,256]{1,0:T(8,128)}, bf16[1024,256]{1,0:T(8,128)(2,1)}) custom-call(bf16[1024,256]{1,0:T(8,128)(2,1)} %get-tuple-element.6.refs_0_, f32[256,256]{1,0:T(8,128)} %get-tuple-element.7.refs_1_, bf16[1024,256]{1,0:T(8,128)(2,1)} %get-tuple-element.8.refs_2_), custom_call_target="tpu_custom_call" | custom-call | tf_op jit(solution)/shard_map/pallas_call | solution.py:770
